TPU v7x, 32 devices: a whole 2x2x4 slice. The times are simulated.
32 devices in a mesh: gx: 2 (over core), gy: 4 (over y, x), gz: 4 (over z).
Axes of the slice: x: 2, y: 2, z: 4, core: 2. Of those that a mesh axis runs over, the one named last changes fastest.
Arguments:
- dual_matrix: float32 [2, 4, 4, 1536, 1536], P('gx', 'gy', 'gz'), may hold values from -1 to 4, as said below
- modes: float32 [2, 4, 4, 6, 1536], P('gx', 'gy', 'gz'), may hold values from -0.15625 to 0.15625
- coarse_rows: float32 [192, 192], P(('gx', 'gy', 'gz')), may hold values from -0.2 to 0.4, as said below
- loads: float32 [2, 4, 4, 8, 6, 128], P('gx', 'gy', 'gz'), may hold values from -40 to 40
- face_counts: int32 [2, 4, 4, 3], replicated, may hold values from 32 to 128
- contact: int32 [2, 4, 4, 6, 128], P('gx', 'gy', 'gz'), may hold values 0 or 1
Outputs:
- multipliers: float32 [2, 4, 4, 8, 6, 128], P('gx', 'gy', 'gz')
- residual: float32 [2, 4, 4, 8, 6, 128], P('gx', 'gy', 'gz')
Inputs may be any that keep to these rules, and one draw needn't show every extreme that they name: `dual_matrix`: every subdomain's matrix is symmetric positive definite. `coarse_rows`: the coarse operator is symmetric positive definite.
All inputs are finite; a program needn't handle non-finite values. No bound on the sum of `contact` on one device may be relied on, other than what follows from the above.
Results may differ from a plain program's by a relative error of at most 0.0003.
Values sent between devices are 32-bit elements; how exact they have to be, the bound alone decides.
A program may use at most 128 MiB of HBM per device.

v0:
```python
import jax
import jax.numpy as jnp
from jax import lax
from jax.sharding import PartitionSpec as P

ITERS = 4
highest = lax.Precision.HIGHEST


def from_behind(block, axis, distance):
    devices = range(lax.axis_size(axis))
    route = [((i - distance) % len(devices), i) for i in devices]
    return lax.ppermute(block, axis, route)


def trade(upper_faces, lower_faces):
    from_below = [
        from_behind(upper_faces[0], "gx", 1),
        from_behind(upper_faces[1], "gy", 1),
        from_behind(upper_faces[2], "gz", 1),
    ]
    from_above = [
        from_behind(lower_faces[0], "gx", -1),
        from_behind(lower_faces[1], "gy", -1),
        from_behind(lower_faces[2], "gz", -1),
    ]
    return (from_below, from_above)


def spread_faces(owned_vec):
    upper_faces = [owned_vec[..., 2 * grid_axis + 1, :] for grid_axis in range(3)]
    lower_faces = [owned_vec[..., 2 * grid_axis, :] for grid_axis in range(3)]
    from_below, from_above = trade(upper_faces, lower_faces)
    faces = []
    for grid_axis in range(3):
        faces.append(jnp.concatenate([from_below[grid_axis], lower_faces[grid_axis]], axis=-1))
        faces.append(jnp.concatenate([upper_faces[grid_axis], from_above[grid_axis]], axis=-1))
    return jnp.stack(faces, axis=-2)


def collect_faces(local_form):
    half_width = local_form.shape[-1] // 2
    upper_faces = [local_form[..., 2 * grid_axis + 1, half_width:] for grid_axis in range(3)]
    lower_faces = [local_form[..., 2 * grid_axis, :half_width] for grid_axis in range(3)]
    from_below, from_above = trade(upper_faces, lower_faces)
    pieces = []
    for grid_axis in range(3):
        pieces.append(local_form[..., 2 * grid_axis, half_width:] + from_below[grid_axis])
        pieces.append(local_form[..., 2 * grid_axis + 1, :half_width] + from_above[grid_axis])
    return jnp.stack(pieces, axis=-2)


def coarse_weights(flattened, own_modes, coarse_rows):
    on_modes = jnp.einsum("jm,km->jk", own_modes, flattened, precision=highest)
    return jnp.dot(
        coarse_rows,
        lax.all_gather(on_modes, ("gx", "gy", "gz"), axis=0, tiled=True),
        precision=highest,
    )


def on_device(dual_matrix, modes, coarse_rows, loads, face_counts, contact):
    half_width = loads.shape[-1]
    case_count = loads.shape[3]
    grid_pos = [lax.axis_index("gx"), lax.axis_index("gy"), lax.axis_index("gz")]
    grid_sizes = [lax.axis_size("gx"), lax.axis_size("gy"), lax.axis_size("gz")]

    def counts_at(where):
        return lax.dynamic_slice(
            face_counts, (where[0], where[1], where[2], 0), (1, 1, 1, 3)
        ).reshape(3)

    own_counts = counts_at(grid_pos)
    positions = jnp.arange(half_width, dtype=jnp.int32)
    own_masks = []
    local_masks = []
    for grid_axis in range(3):
        lower_pos = list(grid_pos)
        lower_pos[grid_axis] = (grid_pos[grid_axis] - 1 + grid_sizes[grid_axis]) % grid_sizes[
            grid_axis
        ]
        lower_count = counts_at(lower_pos)[grid_axis]
        lower_row = (positions < lower_count).astype(jnp.float32)
        upper_row = (positions < own_counts[grid_axis]).astype(jnp.float32)
        own_masks.extend([lower_row, upper_row])
        local_masks.extend(
            [jnp.concatenate([lower_row, lower_row]), jnp.concatenate([upper_row, upper_row])]
        )
    active_own = jnp.stack(own_masks).reshape(1, 1, 1, 1, 6, half_width)
    is_contact = contact[:, :, :, None] == 1
    matrix = dual_matrix[0, 0, 0]
    own_modes = modes[0, 0, 0]

    def local_coarse(local_form):
        flattened = local_form.reshape(case_count, -1)
        weights = coarse_weights(flattened, own_modes, coarse_rows)
        return jnp.einsum("jk,jm->km", weights, own_modes, precision=highest).reshape(
            local_form.shape
        )

    def project(vector):
        return vector - collect_faces(local_coarse(spread_faces(vector))) * active_own

    start_vector = loads * active_own

    def partial_inner(first, second):
        return jnp.sum(first * second, axis=(0, 1, 2, 4, 5))

    multipliers = jnp.zeros(loads.shape, jnp.float32)
    residual = start_vector

    def energy_sum(first, second):
        return lax.psum(partial_inner(first, second), ("gx", "gy", "gz")).reshape(-1, 1, 1)

    precond = project(residual)
    direction = precond
    energy = energy_sum(residual, precond)
    for rounds in range(ITERS):
        local_local_form = spread_faces(direction)
        local_flattened = local_local_form.reshape(case_count, -1)
        dual_image = (
            collect_faces(
                jnp.dot(local_flattened, matrix, precision=highest).reshape(local_local_form.shape)
            )
            * active_own
        )
        curvature = lax.psum(partial_inner(direction, dual_image), ("gx", "gy", "gz")).reshape(
            -1, 1, 1
        )
        step_size = energy / curvature
        updated = multipliers + step_size * direction
        multipliers = jnp.where(is_contact, jnp.maximum(updated, 0.0), updated)
        residual = residual - step_size * dual_image
        if rounds + 1 < ITERS:
            precond = project(residual)
            energy_next = energy_sum(residual, precond)
            direction = precond + energy_next / energy * direction
            energy = energy_next
    return (multipliers, residual)


def solution(mesh):
    return jax.shard_map(
        on_device,
        mesh=mesh,
        in_specs=(
            P("gx", "gy", "gz", None, None),
            P("gx", "gy", "gz", None, None),
            P(("gx", "gy", "gz"), None),
            P("gx", "gy", "gz", None, None, None),
            P(),
            P("gx", "gy", "gz", None, None),
        ),
        out_specs=(P("gx", "gy", "gz", None, None, None), P("gx", "gy", "gz", None, None, None)),
        check_vma=False,
    )
```

profile of v0, /device:TPU:0, one launch (start us, length us, event | category | flops | bytes accessed | tf_op | source)
XLA Modules:
  0.0 787.7 jit_solution(9719686072488246595)
XLA Ops:
  18.8 67.1 %all-gather = f32[32,6,8]{2,1,0:T(8,128)S(1)} all-gather(f32[1,6,8]{2,1,0:T(8,128)S(1)} %bitcast.1086), channel_id=1, replica_groups=mesh['gx'=2,'gy'=4,'gz'=4] {'gx','gy','gz'}, dimensions={0}, use_global_device_ids=true | all-gather | bytes 6336 | tf_op jit(solution)/shard_map/all_gather | solution.py:57
  91.9 3.9 collective-permute-start.11
  95.8 4.1 collective-permute-done.9
  100.8 9.6 %copy.36 = f32[1,1,1,1536,1536]{3,4,2,1,0:T(8,128)} copy(f32[1,1,1,1536,1536]{4,3,2,1,0:T(8,128)} %param.6) | data formatting | bytes 18874368 | tf_op args[0]
  114.7 3.9 collective-permute-start.17
  120.1 10.1 %convolution_bitcast_fusion.6 = f32[1,1,1,8,6,256]{5,3,4,2,1,0:T(8,128)S(1)} fusion(f32[8,1536,1]{1,0,2:T(8,128)S(1)} %bitcast.1078, f32[6,256,1536]{2,1,0:T(8,128)} %bitcast.1070), kind=kOutput, calls=%fused_computation.6 | convolution fusion | flops 226492416 | bytes 9535488 | tf_op jit(solution)/shard_map/dot_general | solution.py:123
  139.4 41.9 %all-reduce = (f32[8]{0:T(128)S(1)}, f32[8]{0:T(128)S(1)}) all-reduce(f32[8]{0:T(128)S(1)} %get-tuple-element.3, f32[8]{0:T(128)S(1)} %get-tuple-element.2), channel_id=1, replica_groups=mesh['gx'=2,'gy'=4,'gz'=4] {'gx','gy','gz'}, use_global_device_ids=true, to_apply=%region_1.2 | all-reduce | flops 16 | bytes 128 | tf_op jit(solution)/shard_map/psum | solution.py:113
  191.2 67.3 %all-gather.1 = f32[32,6,8]{2,1,0:T(8,128)S(1)} all-gather(f32[1,6,8]{2,1,0:T(8,128)S(1)} %bitcast.1087), channel_id=1, replica_groups=mesh['gx'=2,'gy'=4,'gz'=4] {'gx','gy','gz'}, dimensions={0}, use_global_device_ids=true | all-gather | bytes 6336 | tf_op jit(solution)/shard_map/all_gather | solution.py:57
  264.6 3.8 collective-permute-start.35
  272.2 42.4 %psum.58 = f32[8]{0:T(128)S(1)} all-reduce(f32[8]{0:T(128)S(1)} %multiply_reduce_fusion.5), channel_id=1, replica_groups=mesh['gx'=2,'gy'=4,'gz'=4] {'gx','gy','gz'}, use_global_device_ids=true, to_apply=%region_5.6 | all-reduce | flops 8 | bytes 64 | tf_op jit(solution)/shard_map/psum | solution.py:113
  324.7 10.1 %convolution_bitcast_fusion.4 = f32[1,1,1,8,6,256]{5,3,4,2,1,0:T(8,128)S(1)} fusion(f32[8,1536,1]{1,0,2:T(8,128)S(1)} %bitcast.1079, f32[6,256,1536]{2,1,0:T(8,128)} %bitcast.1071), kind=kOutput, calls=%fused_computation.4 | convolution fusion | flops 226492416 | bytes 9535488 | tf_op jit(solution)/shard_map/dot_general | solution.py:123
  343.8 39.2 %psum.59 = f32[8]{0:T(128)S(1)} all-reduce(f32[8]{0:T(128)S(1)} %multiply_reduce_fusion.4), channel_id=1, replica_groups=mesh['gx'=2,'gy'=4,'gz'=4] {'gx','gy','gz'}, use_global_device_ids=true, to_apply=%region_7.8 | all-reduce | flops 8 | bytes 64 | tf_op jit(solution)/shard_map/psum | solution.py:127
  393.0 66.9 %all-gather.2 = f32[32,6,8]{2,1,0:T(8,128)S(1)} all-gather(f32[1,6,8]{2,1,0:T(8,128)S(1)} %bitcast.1088), channel_id=1, replica_groups=mesh['gx'=2,'gy'=4,'gz'=4] {'gx','gy','gz'}, dimensions={0}, use_global_device_ids=true | all-gather | bytes 6336 | tf_op jit(solution)/shard_map/all_gather | solution.py:57
  466.0 3.8 collective-permute-start.59
  469.8 4.1 collective-permute-done.57
  474.1 42.4 %psum.60 = f32[8]{0:T(128)S(1)} all-reduce(f32[8]{0:T(128)S(1)} %multiply_reduce_fusion.3), channel_id=1, replica_groups=mesh['gx'=2,'gy'=4,'gz'=4] {'gx','gy','gz'}, use_global_device_ids=true, to_apply=%region_9.10 | all-reduce | flops 8 | bytes 64 | tf_op jit(solution)/shard_map/psum | solution.py:113
  526.6 10.1 %convolution_bitcast_fusion.2 = f32[1,1,1,8,6,256]{5,3,4,2,1,0:T(8,128)S(1)} fusion(f32[8,1536,1]{1,0,2:T(8,128)S(1)} %bitcast.1080, f32[6,256,1536]{2,1,0:T(8,128)} %bitcast.1072), kind=kOutput, calls=%fused_computation.2 | convolution fusion | flops 226492416 | bytes 9535488 | tf_op jit(solution)/shard_map/dot_general | solution.py:123
  545.7 39.2 %psum.61 = f32[8]{0:T(128)S(1)} all-reduce(f32[8]{0:T(128)S(1)} %multiply_reduce_fusion.2), channel_id=1, replica_groups=mesh['gx'=2,'gy'=4,'gz'=4] {'gx','gy','gz'}, use_global_device_ids=true, to_apply=%region_11.12 | all-reduce | flops 8 | bytes 64 | tf_op jit(solution)/shard_map/psum | solution.py:127
  594.9 66.9 %all-gather.3 = f32[32,6,8]{2,1,0:T(8,128)S(1)} all-gather(f32[1,6,8]{2,1,0:T(8,128)S(1)} %bitcast.1089), channel_id=1, replica_groups=mesh['gx'=2,'gy'=4,'gz'=4] {'gx','gy','gz'}, dimensions={0}, use_global_device_ids=true | all-gather | bytes 6336 | tf_op jit(solution)/shard_map/all_gather | solution.py:57
  667.9 3.8 collective-permute-start.83
  671.7 4.1 collective-permute-done.81
  676.0 42.4 %psum.62 = f32[8]{0:T(128)S(1)} all-reduce(f32[8]{0:T(128)S(1)} %multiply_reduce_fusion.1), channel_id=1, replica_groups=mesh['gx'=2,'gy'=4,'gz'=4] {'gx','gy','gz'}, use_global_device_ids=true, to_apply=%region_13.14 | all-reduce | flops 8 | bytes 64 | tf_op jit(solution)/shard_map/psum | solution.py:113
  728.5 10.1 %convolution_bitcast_fusion = f32[1,1,1,8,6,256]{5,3,4,2,1,0:T(8,128)S(1)} fusion(f32[8,1536,1]{1,0,2:T(8,128)S(1)} %bitcast.1081, f32[6,256,1536]{2,1,0:T(8,128)} %bitcast.1073), kind=kOutput, calls=%fused_computation | convolution fusion | flops 226492416 | bytes 9535488 | tf_op jit(solution)/shard_map/dot_general | solution.py:123
  747.7 39.3 %psum.63 = f32[8]{0:T(128)S(1)} all-reduce(f32[8]{0:T(128)S(1)} %multiply_reduce_fusion), channel_id=1, replica_groups=mesh['gx'=2,'gy'=4,'gz'=4] {'gx','gy','gz'}, use_global_device_ids=true, to_apply=%region_15.16 | all-reduce | flops 8 | bytes 64 | tf_op jit(solution)/shard_map/psum | solution.py:127
  (356 shorter events, 149.5 us)
Async XLA Ops:
  7.3 8.9 %collective-permute-start.1 = (f32[1,1,1,8,128]{4,3,2,1,0:T(8,128)S(1)}, f32[1,1,1,8,128]{4,3,2,1,0:T(8,128)S(1)}, u32[]{:S(2)}, u32[]{:S(2)}) collective-permute-start(f32[1,1,1,8,128]{4,3,2,1,0:T(8,128)S(1)} %get-tuple-element.100), channel_id=1, source_target_pairs={{16,0},{0,16},{17,1},{1,17},{18,2},{2,18},{19,3},{3,19},{20,4},{4,... | collective-permute-start | bytes 12296 | tf_op jit(solution)/shard_map/ppermute | solution.py:13
  7.4 8.8 %collective-permute-start.2 = (f32[1,1,1,8,128]{4,3,2,1,0:T(8,128)S(1)}, f32[1,1,1,8,128]{4,3,2,1,0:T(8,128)S(1)}, u32[]{:S(2)}, u32[]{:S(2)}) collective-permute-start(f32[1,1,1,8,128]{4,3,2,1,0:T(8,128)S(1)} %get-tuple-element.99), channel_id=1, source_target_pairs={{12,0},{0,4},{4,8},{8,12},{13,1},{1,5},{5,9},{9,13},{14,2},{2,6},{... | collective-permute-start | bytes 12296 | tf_op jit(solution)/shard_map/ppermute | solution.py:13
  90.6 9.4 %collective-permute-start.9 = (f32[1,1,1,8,128]{4,3,2,1,0:T(8,128)S(1)}, f32[1,1,1,8,128]{4,3,2,1,0:T(8,128)S(1)}, u32[]{:S(2)}, u32[]{:S(2)}) collective-permute-start(f32[1,1,1,8,128]{4,3,2,1,0:T(8,128)S(1)} %get-tuple-element.50), channel_id=1, source_target_pairs={{4,0},{8,4},{12,8},{0,12},{5,1},{9,5},{13,9},{1,13},{6,2},{10,6},{... | collective-permute-start | bytes 12296 | tf_op jit(solution)/shard_map/ppermute | solution.py:13
  91.9 8.0 %collective-permute-start.10 = (f32[1,1,1,8,128]{4,3,2,1,0:T(8,128)S(1)}, f32[1,1,1,8,128]{4,3,2,1,0:T(8,128)S(1)}, u32[]{:S(2)}, u32[]{:S(2)}) collective-permute-start(f32[1,1,1,8,128]{4,3,2,1,0:T(8,128)S(1)} %get-tuple-element.49), channel_id=1, source_target_pairs={{3,0},{0,1},{1,2},{2,3},{7,4},{4,5},{5,6},{6,7},{11,8},{8,9},{9,10... | collective-permute-start | bytes 12296 | tf_op jit(solution)/shard_map/ppermute | solution.py:13
  91.9 8.0 %collective-permute-start.11 = (f32[1,1,1,8,128]{4,3,2,1,0:T(8,128)S(1)}, f32[1,1,1,8,128]{4,3,2,1,0:T(8,128)S(1)}, u32[]{:S(2)}, u32[]{:S(2)}) collective-permute-start(f32[1,1,1,8,128]{4,3,2,1,0:T(8,128)S(1)} %get-tuple-element.48), channel_id=1, source_target_pairs={{1,0},{2,1},{3,2},{0,3},{5,4},{6,5},{7,6},{4,7},{9,8},{10,9},{11,1... | collective-permute-start | bytes 12296 | tf_op jit(solution)/shard_map/ppermute | solution.py:13
  100.7 14.0 %collective-permute-start.12 = (f32[1,1,1,8,128]{4,3,2,1,0:T(8,128)S(1)}, f32[1,1,1,8,128]{4,3,2,1,0:T(8,128)S(1)}, u32[]{:S(2)}, u32[]{:S(2)}) collective-permute-start(f32[1,1,1,8,128]{4,3,2,1,0:T(8,128)S(1)} %get-tuple-element.95), channel_id=1, source_target_pairs={{16,0},{0,16},{17,1},{1,17},{18,2},{2,18},{19,3},{3,19},{20,4},{4,... | collective-permute-start | bytes 12296 | tf_op jit(solution)/shard_map/ppermute | solution.py:13
  110.5 8.1 %collective-permute-start.13 = (f32[1,1,1,8,128]{4,3,2,1,0:T(8,128)S(1)}, f32[1,1,1,8,128]{4,3,2,1,0:T(8,128)S(1)}, u32[]{:S(2)}, u32[]{:S(2)}) collective-permute-start(f32[1,1,1,8,128]{4,3,2,1,0:T(8,128)S(1)} %get-tuple-element.94), channel_id=1, source_target_pairs={{16,0},{0,16},{17,1},{1,17},{18,2},{2,18},{19,3},{3,19},{20,4},{4,... | collective-permute-start | bytes 12296 | tf_op jit(solution)/shard_map/ppermute | solution.py:13
  110.9 7.7 collective-permute-start.14
  181.4 8.0 %collective-permute-start.25 = (f32[1,1,1,8,128]{4,3,2,1,0:T(8,128)S(1)}, f32[1,1,1,8,128]{4,3,2,1,0:T(8,128)S(1)}, u32[]{:S(2)}, u32[]{:S(2)}) collective-permute-start(f32[1,1,1,8,128]{4,3,2,1,0:T(8,128)S(1)} %get-tuple-element.88), channel_id=1, source_target_pairs={{16,0},{0,16},{17,1},{1,17},{18,2},{2,18},{19,3},{3,19},{20,4},{4,... | collective-permute-start | bytes 12296 | tf_op jit(solution)/shard_map/ppermute | solution.py:13
  262.7 9.4 %collective-permute-start.33 = (f32[1,1,1,8,128]{4,3,2,1,0:T(8,128)S(1)}, f32[1,1,1,8,128]{4,3,2,1,0:T(8,128)S(1)}, u32[]{:S(2)}, u32[]{:S(2)}) collective-permute-start(f32[1,1,1,8,128]{4,3,2,1,0:T(8,128)S(1)} %get-tuple-element.38), channel_id=1, source_target_pairs={{4,0},{8,4},{12,8},{0,12},{5,1},{9,5},{13,9},{1,13},{6,2},{10,6},{... | collective-permute-start | bytes 12296 | tf_op jit(solution)/shard_map/ppermute | solution.py:13
  314.7 8.1 %collective-permute-start.37 = (f32[1,1,1,8,128]{4,3,2,1,0:T(8,128)S(1)}, f32[1,1,1,8,128]{4,3,2,1,0:T(8,128)S(1)}, u32[]{:S(2)}, u32[]{:S(2)}) collective-permute-start(f32[1,1,1,8,128]{4,3,2,1,0:T(8,128)S(1)} %get-tuple-element.82), channel_id=1, source_target_pairs={{16,0},{0,16},{17,1},{1,17},{18,2},{2,18},{19,3},{3,19},{20,4},{4,... | collective-permute-start | bytes 12296 | tf_op jit(solution)/shard_map/ppermute | solution.py:13
  315.2 7.6 collective-permute-start.38
  383.2 7.5 collective-permute-start.49
  464.5 9.4 %collective-permute-start.57 = (f32[1,1,1,8,128]{4,3,2,1,0:T(8,128)S(1)}, f32[1,1,1,8,128]{4,3,2,1,0:T(8,128)S(1)}, u32[]{:S(2)}, u32[]{:S(2)}) collective-permute-start(f32[1,1,1,8,128]{4,3,2,1,0:T(8,128)S(1)} %get-tuple-element.26), channel_id=1, source_target_pairs={{4,0},{8,4},{12,8},{0,12},{5,1},{9,5},{13,9},{1,13},{6,2},{10,6},{... | collective-permute-start | bytes 12296 | tf_op jit(solution)/shard_map/ppermute | solution.py:13
  466.0 8.0 %collective-permute-start.58 = (f32[1,1,1,8,128]{4,3,2,1,0:T(8,128)S(1)}, f32[1,1,1,8,128]{4,3,2,1,0:T(8,128)S(1)}, u32[]{:S(2)}, u32[]{:S(2)}) collective-permute-start(f32[1,1,1,8,128]{4,3,2,1,0:T(8,128)S(1)} %get-tuple-element.25), channel_id=1, source_target_pairs={{3,0},{0,1},{1,2},{2,3},{7,4},{4,5},{5,6},{6,7},{11,8},{8,9},{9,10... | collective-permute-start | bytes 12296 | tf_op jit(solution)/shard_map/ppermute | solution.py:13
  466.0 8.0 %collective-permute-start.59 = (f32[1,1,1,8,128]{4,3,2,1,0:T(8,128)S(1)}, f32[1,1,1,8,128]{4,3,2,1,0:T(8,128)S(1)}, u32[]{:S(2)}, u32[]{:S(2)}) collective-permute-start(f32[1,1,1,8,128]{4,3,2,1,0:T(8,128)S(1)} %get-tuple-element.24), channel_id=1, source_target_pairs={{1,0},{2,1},{3,2},{0,3},{5,4},{6,5},{7,6},{4,7},{9,8},{10,9},{11,1... | collective-permute-start | bytes 12296 | tf_op jit(solution)/shard_map/ppermute | solution.py:13
  516.6 8.1 %collective-permute-start.61 = (f32[1,1,1,8,128]{4,3,2,1,0:T(8,128)S(1)}, f32[1,1,1,8,128]{4,3,2,1,0:T(8,128)S(1)}, u32[]{:S(2)}, u32[]{:S(2)}) collective-permute-start(f32[1,1,1,8,128]{4,3,2,1,0:T(8,128)S(1)} %get-tuple-element.70), channel_id=1, source_target_pairs={{16,0},{0,16},{17,1},{1,17},{18,2},{2,18},{19,3},{3,19},{20,4},{4,... | collective-permute-start | bytes 12296 | tf_op jit(solution)/shard_map/ppermute | solution.py:13
  517.1 7.6 collective-permute-start.62
  585.1 7.5 collective-permute-start.73
  666.4 9.4 %collective-permute-start.81 = (f32[1,1,1,8,128]{4,3,2,1,0:T(8,128)S(1)}, f32[1,1,1,8,128]{4,3,2,1,0:T(8,128)S(1)}, u32[]{:S(2)}, u32[]{:S(2)}) collective-permute-start(f32[1,1,1,8,128]{4,3,2,1,0:T(8,128)S(1)} %get-tuple-element.14), channel_id=1, source_target_pairs={{4,0},{8,4},{12,8},{0,12},{5,1},{9,5},{13,9},{1,13},{6,2},{10,6},{... | collective-permute-start | bytes 12296 | tf_op jit(solution)/shard_map/ppermute | solution.py:13
  667.9 8.0 %collective-permute-start.82 = (f32[1,1,1,8,128]{4,3,2,1,0:T(8,128)S(1)}, f32[1,1,1,8,128]{4,3,2,1,0:T(8,128)S(1)}, u32[]{:S(2)}, u32[]{:S(2)}) collective-permute-start(f32[1,1,1,8,128]{4,3,2,1,0:T(8,128)S(1)} %get-tuple-element.13), channel_id=1, source_target_pairs={{3,0},{0,1},{1,2},{2,3},{7,4},{4,5},{5,6},{6,7},{11,8},{8,9},{9,10... | collective-permute-start | bytes 12296 | tf_op jit(solution)/shard_map/ppermute | solution.py:13
  667.9 8.0 %collective-permute-start.83 = (f32[1,1,1,8,128]{4,3,2,1,0:T(8,128)S(1)}, f32[1,1,1,8,128]{4,3,2,1,0:T(8,128)S(1)}, u32[]{:S(2)}, u32[]{:S(2)}) collective-permute-start(f32[1,1,1,8,128]{4,3,2,1,0:T(8,128)S(1)} %get-tuple-element.12), channel_id=1, source_target_pairs={{1,0},{2,1},{3,2},{0,3},{5,4},{6,5},{7,6},{4,7},{9,8},{10,9},{11,1... | collective-permute-start | bytes 12296 | tf_op jit(solution)/shard_map/ppermute | solution.py:13
  718.5 8.1 %collective-permute-start.85 = (f32[1,1,1,8,128]{4,3,2,1,0:T(8,128)S(1)}, f32[1,1,1,8,128]{4,3,2,1,0:T(8,128)S(1)}, u32[]{:S(2)}, u32[]{:S(2)}) collective-permute-start(f32[1,1,1,8,128]{4,3,2,1,0:T(8,128)S(1)} %get-tuple-element.58), channel_id=1, source_target_pairs={{16,0},{0,16},{17,1},{1,17},{18,2},{2,18},{19,3},{3,19},{20,4},{4,... | collective-permute-start | bytes 12296 | tf_op jit(solution)/shard_map/ppermute | solution.py:13
  719.0 7.6 collective-permute-start.86
  (76 other events, 816.4 us)
where the time goes:
time: 789 us; the launch traced here: 788 us
  blocking collectives  555 us (70%)
  starting transfers between devices  131 us (17%)
  matrix products  43.7 us (6%)
  waiting for transfers between devices  36.2 us (5%)
  local copies, waits for them, and re-layouts  12.5 us (2%)
    all_gather x4, blocking collectives, coarse_weights(): lax.all_gather(on_modes, ('gx', 'gy', 'gz'), axis=0, tiled=True)  268 us
    psum x4, blocking collectives, energy_sum(): lax.psum(partial_inner(first, second), ('gx', 'gy', 'gz')).reshape(-1, 1, 1)  169 us
    ppermute x96, starting transfers between devices, from_behind(): return lax.ppermute(block, axis, route)  131 us
    psum x3, blocking collectives, on_device(): lax.psum(partial_inner(direction, dual_image), ('gx', 'gy', 'gz'))  118 us
    dot_general x4, matrix products, on_device(): jnp.dot(local_flattened, matrix, precision=highest)  40.3 us
    ppermute x96, waiting for transfers between devices, from_behind(): return lax.ppermute(block, axis, route)  36.2 us
  transfers between devices with their start and end apart: 96, of which 24 were waited for; matrix products, arithmetic and copies ran while one was open for 1% of the time, Pallas kernels for 0%

commit v1 on v0

--- a/solution.py
+++ b/solution.py
@@ -2,6 +2,7 @@
 import jax.numpy as jnp
 from jax import lax
 from jax.sharding import PartitionSpec as P
+from jax.lax import psum
 
 ITERS = 4
 highest = lax.Precision.HIGHEST
@@ -110,7 +111,9 @@
     residual = start_vector
 
     def energy_sum(first, second):
-        return lax.psum(partial_inner(first, second), ("gx", "gy", "gz")).reshape(-1, 1, 1)
+        return psum(
+            psum(partial_inner(first, second), axis_name=("gy", "gz")), axis_name="gx"
+        ).reshape(-1, 1, 1)
 
     precond = project(residual)
     direction = precond

time: 789 us -> 838 us (1.062)
  blocking collectives: 555 us -> 607 us
    psum x3 -> x4, blocking collectives: 118 us -> 155 us  [on_device(): lax.psum(partial_inner(direction, dual_image), ('gx', 'gy', 'gz'))]
    psum x4 -> x8, blocking collectives: 169 us -> 184 us  [the longest x4 174 us: energy_sum(): psum(partial_inner(first, second), axis_name=('gy', 'gz'))]
  transfers between devices with their start and end apart: 96 -> 96, of which waited for: 24 -> 20; matrix products, arithmetic and copies ran while one was open for 1% -> 1% of each run, Pallas kernels for 0% -> 0%
where the time goes in v1:
time: 838 us; the launch traced here: 837 us
  blocking collectives  607 us (72%)
  starting transfers between devices  128 us (15%)
  matrix products  43.7 us (5%)
  waiting for transfers between devices  35.9 us (4%)
  local copies, waits for them, and re-layouts  12.5 us (1%)
    all_gather x4, blocking collectives, coarse_weights(): lax.all_gather(on_modes, ('gx', 'gy', 'gz'), axis=0, tiled=True)  268 us
    psum x4, blocking collectives, energy_sum(): psum(partial_inner(first, second), axis_name=('gy', 'gz'))  174 us
    psum x4, blocking collectives, on_device(): lax.psum(partial_inner(direction, dual_image), ('gx', 'gy', 'gz'))  155 us
    ppermute x96, starting transfers between devices, from_behind(): return lax.ppermute(block, axis, route)  128 us
    dot_general x4, matrix products, on_device(): jnp.dot(local_flattened, matrix, precision=highest)  40.3 us
    ppermute x96, waiting for transfers between devices, from_behind(): return lax.ppermute(block, axis, route)  35.9 us
  transfers between devices with their start and end apart: 96, of which 20 were waited for; matrix products, arithmetic and copies ran while one was open for 1% of the time, Pallas kernels for 0%

profile of v1, /device:TPU:0, one launch (start us, length us, event | category | flops | bytes accessed | tf_op | source)
XLA Modules:
  0.0 836.5 jit_solution(18280855844547458978)
XLA Ops:
  18.8 67.1 %all-gather = f32[32,6,8]{2,1,0:T(8,128)S(1)} all-gather(f32[1,6,8]{2,1,0:T(8,128)S(1)} %bitcast.1086), channel_id=1, replica_groups=mesh['gx'=2,'gy'=4,'gz'=4] {'gx','gy','gz'}, dimensions={0}, use_global_device_ids=true | all-gather | bytes 6336 | tf_op jit(solution)/shard_map/all_gather | solution.py:58
  91.9 3.9 collective-permute-start.11
  95.7 4.1 collective-permute-done.9
  100.8 9.7 %copy.36 = f32[1,1,1,1536,1536]{3,4,2,1,0:T(8,128)} copy(f32[1,1,1,1536,1536]{4,3,2,1,0:T(8,128)} %param.6) | data formatting | bytes 18874368 | tf_op args[0]
  114.7 3.9 collective-permute-start.17
  120.1 10.1 %convolution_bitcast_fusion.6 = f32[1,1,1,8,6,256]{5,3,4,2,1,0:T(8,128)S(1)} fusion(f32[8,1536,1]{1,0,2:T(8,128)S(1)} %bitcast.1078, f32[6,256,1536]{2,1,0:T(8,128)} %bitcast.1070), kind=kOutput, calls=%fused_computation.6 | convolution fusion | flops 226492416 | bytes 9535488 | tf_op jit(solution)/shard_map/dot_general | solution.py:126
  139.3 42.9 %psum.84 = f32[8]{0:T(128)S(1)} all-reduce(f32[8]{0:T(128)S(1)} %get-tuple-element.3), channel_id=1, replica_groups=mesh['gx'=2,'gy'=4,'gz'=4] {'gy','gz'}, use_global_device_ids=true, to_apply=%region_1.2 | all-reduce | flops 8 | bytes 64 | tf_op jit(solution)/shard_map/psum | solution.py:115
  184.6 36.8 %psum.86 = f32[8]{0:T(128)S(1)} all-reduce(f32[8]{0:T(128)S(1)} %get-tuple-element.2), channel_id=1, replica_groups=mesh['gx'=2,'gy'=4,'gz'=4] {'gx','gy','gz'}, use_global_device_ids=true, to_apply=%region_4.5 | all-reduce | flops 8 | bytes 64 | tf_op jit(solution)/shard_map/psum | solution.py:130
  232.0 66.3 %all-gather.1 = f32[32,6,8]{2,1,0:T(8,128)S(1)} all-gather(f32[1,6,8]{2,1,0:T(8,128)S(1)} %bitcast.1087), channel_id=1, replica_groups=mesh['gx'=2,'gy'=4,'gz'=4] {'gx','gy','gz'}, dimensions={0}, use_global_device_ids=true | all-gather | bytes 6336 | tf_op jit(solution)/shard_map/all_gather | solution.py:58
  308.2 4.0 collective-permute-done.33
  312.4 43.7 %psum.87 = f32[8]{0:T(128)S(1)} all-reduce(f32[8]{0:T(128)S(1)} %multiply_reduce_fusion.5), channel_id=1, replica_groups=mesh['gx'=2,'gy'=4,'gz'=4] {'gy','gz'}, use_global_device_ids=true, to_apply=%region_6.7 | all-reduce | flops 8 | bytes 64 | tf_op jit(solution)/shard_map/psum | solution.py:115
  362.2 3.8 collective-permute-start.41
  367.6 10.1 %convolution_bitcast_fusion.4 = f32[1,1,1,8,6,256]{5,3,4,2,1,0:T(8,128)S(1)} fusion(f32[8,1536,1]{1,0,2:T(8,128)S(1)} %bitcast.1079, f32[6,256,1536]{2,1,0:T(8,128)} %bitcast.1071), kind=kOutput, calls=%fused_computation.4 | convolution fusion | flops 226492416 | bytes 9535488 | tf_op jit(solution)/shard_map/dot_general | solution.py:126
  386.7 39.5 %psum.89 = f32[8]{0:T(128)S(1)} all-reduce(f32[8]{0:T(128)S(1)} %multiply_reduce_fusion.4), channel_id=1, replica_groups=mesh['gx'=2,'gy'=4,'gz'=4] {'gx','gy','gz'}, use_global_device_ids=true, to_apply=%region_9.10 | all-reduce | flops 8 | bytes 64 | tf_op jit(solution)/shard_map/psum | solution.py:130
  435.7 67.3 %all-gather.2 = f32[32,6,8]{2,1,0:T(8,128)S(1)} all-gather(f32[1,6,8]{2,1,0:T(8,128)S(1)} %bitcast.1088), channel_id=1, replica_groups=mesh['gx'=2,'gy'=4,'gz'=4] {'gx','gy','gz'}, dimensions={0}, use_global_device_ids=true | all-gather | bytes 6336 | tf_op jit(solution)/shard_map/all_gather | solution.py:58
  512.9 4.1 collective-permute-done.57
  517.2 43.7 %psum.90 = f32[8]{0:T(128)S(1)} all-reduce(f32[8]{0:T(128)S(1)} %multiply_reduce_fusion.3), channel_id=1, replica_groups=mesh['gx'=2,'gy'=4,'gz'=4] {'gy','gz'}, use_global_device_ids=true, to_apply=%region_11.12 | all-reduce | flops 8 | bytes 64 | tf_op jit(solution)/shard_map/psum | solution.py:115
  572.3 10.1 %convolution_bitcast_fusion.2 = f32[1,1,1,8,6,256]{5,3,4,2,1,0:T(8,128)S(1)} fusion(f32[8,1536,1]{1,0,2:T(8,128)S(1)} %bitcast.1080, f32[6,256,1536]{2,1,0:T(8,128)} %bitcast.1072), kind=kOutput, calls=%fused_computation.2 | convolution fusion | flops 226492416 | bytes 9535488 | tf_op jit(solution)/shard_map/dot_general | solution.py:126
  591.5 39.5 %psum.92 = f32[8]{0:T(128)S(1)} all-reduce(f32[8]{0:T(128)S(1)} %multiply_reduce_fusion.2), channel_id=1, replica_groups=mesh['gx'=2,'gy'=4,'gz'=4] {'gx','gy','gz'}, use_global_device_ids=true, to_apply=%region_14.15 | all-reduce | flops 8 | bytes 64 | tf_op jit(solution)/shard_map/psum | solution.py:130
  640.5 67.3 %all-gather.3 = f32[32,6,8]{2,1,0:T(8,128)S(1)} all-gather(f32[1,6,8]{2,1,0:T(8,128)S(1)} %bitcast.1089), channel_id=1, replica_groups=mesh['gx'=2,'gy'=4,'gz'=4] {'gx','gy','gz'}, dimensions={0}, use_global_device_ids=true | all-gather | bytes 6336 | tf_op jit(solution)/shard_map/all_gather | solution.py:58
  717.7 4.1 collective-permute-done.81
  721.9 43.7 %psum.93 = f32[8]{0:T(128)S(1)} all-reduce(f32[8]{0:T(128)S(1)} %multiply_reduce_fusion.1), channel_id=1, replica_groups=mesh['gx'=2,'gy'=4,'gz'=4] {'gy','gz'}, use_global_device_ids=true, to_apply=%region_16.17 | all-reduce | flops 8 | bytes 64 | tf_op jit(solution)/shard_map/psum | solution.py:115
  777.1 10.1 %convolution_bitcast_fusion = f32[1,1,1,8,6,256]{5,3,4,2,1,0:T(8,128)S(1)} fusion(f32[8,1536,1]{1,0,2:T(8,128)S(1)} %bitcast.1081, f32[6,256,1536]{2,1,0:T(8,128)} %bitcast.1073), kind=kOutput, calls=%fused_computation | convolution fusion | flops 226492416 | bytes 9535488 | tf_op jit(solution)/shard_map/dot_general | solution.py:126
  796.3 39.5 %psum.95 = f32[8]{0:T(128)S(1)} all-reduce(f32[8]{0:T(128)S(1)} %multiply_reduce_fusion), channel_id=1, replica_groups=mesh['gx'=2,'gy'=4,'gz'=4] {'gx','gy','gz'}, use_global_device_ids=true, to_apply=%region_19.20 | all-reduce | flops 8 | bytes 64 | tf_op jit(solution)/shard_map/psum | solution.py:130
  (361 shorter events, 159.7 us)
Async XLA Ops:
  7.3 8.9 %collective-permute-start.1 = (f32[1,1,1,8,128]{4,3,2,1,0:T(8,128)S(1)}, f32[1,1,1,8,128]{4,3,2,1,0:T(8,128)S(1)}, u32[]{:S(2)}, u32[]{:S(2)}) collective-permute-start(f32[1,1,1,8,128]{4,3,2,1,0:T(8,128)S(1)} %get-tuple-element.98), channel_id=1, source_target_pairs={{16,0},{0,16},{17,1},{1,17},{18,2},{2,18},{19,3},{3,19},{20,4},{4,... | collective-permute-start | bytes 12296 | tf_op jit(solution)/shard_map/ppermute | solution.py:14
  7.4 8.8 %collective-permute-start.2 = (f32[1,1,1,8,128]{4,3,2,1,0:T(8,128)S(1)}, f32[1,1,1,8,128]{4,3,2,1,0:T(8,128)S(1)}, u32[]{:S(2)}, u32[]{:S(2)}) collective-permute-start(f32[1,1,1,8,128]{4,3,2,1,0:T(8,128)S(1)} %get-tuple-element.97), channel_id=1, source_target_pairs={{12,0},{0,4},{4,8},{8,12},{13,1},{1,5},{5,9},{9,13},{14,2},{2,6},{... | collective-permute-start | bytes 12296 | tf_op jit(solution)/shard_map/ppermute | solution.py:14
  90.5 9.4 %collective-permute-start.9 = (f32[1,1,1,8,128]{4,3,2,1,0:T(8,128)S(1)}, f32[1,1,1,8,128]{4,3,2,1,0:T(8,128)S(1)}, u32[]{:S(2)}, u32[]{:S(2)}) collective-permute-start(f32[1,1,1,8,128]{4,3,2,1,0:T(8,128)S(1)} %get-tuple-element.48), channel_id=1, source_target_pairs={{4,0},{8,4},{12,8},{0,12},{5,1},{9,5},{13,9},{1,13},{6,2},{10,6},{... | collective-permute-start | bytes 12296 | tf_op jit(solution)/shard_map/ppermute | solution.py:14
  91.8 8.0 collective-permute-start.10
  91.9 8.0 collective-permute-start.11
  100.7 14.0 %collective-permute-start.12 = (f32[1,1,1,8,128]{4,3,2,1,0:T(8,128)S(1)}, f32[1,1,1,8,128]{4,3,2,1,0:T(8,128)S(1)}, u32[]{:S(2)}, u32[]{:S(2)}) collective-permute-start(f32[1,1,1,8,128]{4,3,2,1,0:T(8,128)S(1)} %get-tuple-element.93), channel_id=1, source_target_pairs={{16,0},{0,16},{17,1},{1,17},{18,2},{2,18},{19,3},{3,19},{20,4},{4,... | collective-permute-start | bytes 12296 | tf_op jit(solution)/shard_map/ppermute | solution.py:14
  110.4 8.1 collective-permute-start.13
  110.9 7.7 collective-permute-start.14
  130.3 7.4 collective-permute-start.19
  221.6 7.6 collective-permute-start.25
  302.9 9.4 %collective-permute-start.33 = (f32[1,1,1,8,128]{4,3,2,1,0:T(8,128)S(1)}, f32[1,1,1,8,128]{4,3,2,1,0:T(8,128)S(1)}, u32[]{:S(2)}, u32[]{:S(2)}) collective-permute-start(f32[1,1,1,8,128]{4,3,2,1,0:T(8,128)S(1)} %get-tuple-element.36), channel_id=1, source_target_pairs={{4,0},{8,4},{12,8},{0,12},{5,1},{9,5},{13,9},{1,13},{6,2},{10,6},{... | collective-permute-start | bytes 12296 | tf_op jit(solution)/shard_map/ppermute | solution.py:14
  304.3 7.9 collective-permute-start.34
  304.4 7.9 collective-permute-start.35
  377.8 7.3 collective-permute-start.43
  426.3 7.5 collective-permute-start.49
  507.6 9.4 %collective-permute-start.57 = (f32[1,1,1,8,128]{4,3,2,1,0:T(8,128)S(1)}, f32[1,1,1,8,128]{4,3,2,1,0:T(8,128)S(1)}, u32[]{:S(2)}, u32[]{:S(2)}) collective-permute-start(f32[1,1,1,8,128]{4,3,2,1,0:T(8,128)S(1)} %get-tuple-element.24), channel_id=1, source_target_pairs={{4,0},{8,4},{12,8},{0,12},{5,1},{9,5},{13,9},{1,13},{6,2},{10,6},{... | collective-permute-start | bytes 12296 | tf_op jit(solution)/shard_map/ppermute | solution.py:14
  509.1 7.9 collective-permute-start.58
  509.1 8.0 collective-permute-start.59
  582.5 7.3 collective-permute-start.67
  631.1 7.5 collective-permute-start.73
  712.4 9.4 %collective-permute-start.81 = (f32[1,1,1,8,128]{4,3,2,1,0:T(8,128)S(1)}, f32[1,1,1,8,128]{4,3,2,1,0:T(8,128)S(1)}, u32[]{:S(2)}, u32[]{:S(2)}) collective-permute-start(f32[1,1,1,8,128]{4,3,2,1,0:T(8,128)S(1)} %get-tuple-element.12), channel_id=1, source_target_pairs={{4,0},{8,4},{12,8},{0,12},{5,1},{9,5},{13,9},{1,13},{6,2},{10,6},{... | collective-permute-start | bytes 12296 | tf_op jit(solution)/shard_map/ppermute | solution.py:14
  713.8 7.9 collective-permute-start.82
  713.8 7.9 collective-permute-start.83
  787.3 7.3 collective-permute-start.91
  (76 other events, 859.4 us)
